TPU v7x, 32 devices: a whole 2x2x4 slice. The times are simulated.
32 devices in a mesh: dp: 2 (over x), ctx: 8 (over z, y), tp: 2 (over core).
Axes of the slice: x: 2, y: 2, z: 4, core: 2. Of those that a mesh axis runs over, the one named last changes fastest.
Arguments:
- hidden_in: bfloat16 [2, 2, 1024, 1024], P(None, 'dp', 'ctx'), may hold values from -6 to 6
- lengths: int32 [2, 2], P(None, 'dp'), may hold values from 256 to 1024, as said below
- positions: int32 [2, 2, 1024], P(None, 'dp', 'ctx'), may hold values from 0 to 3069, as said below
- attn_gain: bfloat16 [1024], P(('dp', 'ctx')), may hold values from 0.099609375 to 1.8984375
- w_query: bfloat16 [1024, 1024], P(('dp', 'ctx'), 'tp'), may hold values from -0.1875 to 0.1875
- w_key: bfloat16 [1024, 512], P(('dp', 'ctx'), 'tp'), may hold values from -0.1875 to 0.1875
- w_value: bfloat16 [1024, 512], P(('dp', 'ctx'), 'tp'), may hold values from -0.1875 to 0.1875
- q_gain: bfloat16 [64], replicated, may hold values from 0.099609375 to 1.8984375
- k_gain: bfloat16 [64], replicated, may hold values from 0.099609375 to 1.8984375
- w_output: bfloat16 [1024, 1024], P('tp', ('dp', 'ctx')), may hold values from -1.5 to 1.5
- ffn_gain: bfloat16 [1024], P(('dp', 'ctx')), may hold values from 0.099609375 to 1.8984375
- w_gate: bfloat16 [1024, 4608], P(('dp', 'ctx'), 'tp'), may hold values from -0.1875 to 0.1875
- w_up: bfloat16 [1024, 4608], P(('dp', 'ctx'), 'tp'), may hold values from -0.1875 to 0.1875
- w_down: bfloat16 [4608, 1024], P('tp', ('dp', 'ctx')), may hold values from -0.09375 to 0.09375
- grad_out: bfloat16 [2, 2, 1024, 1024], P(None, 'dp', 'ctx'), may hold values from -6 to 6
Outputs:
- out_hidden: bfloat16 [2, 2, 1024, 1024], P(None, 'dp', 'ctx')
- grad_hidden: bfloat16 [2, 2, 1024, 1024], P(None, 'dp', 'ctx')
- grad_attn_gain: float32 [1024], P(('dp', 'ctx'))
- grad_w_query: float32 [1024, 1024], P(('dp', 'ctx'), 'tp')
- grad_w_key: float32 [1024, 512], P(('dp', 'ctx'), 'tp')
- grad_w_value: float32 [1024, 512], P(('dp', 'ctx'), 'tp')
- grad_q_gain: float32 [64], replicated
- grad_k_gain: float32 [64], replicated
- grad_w_output: float32 [1024, 1024], P('tp', ('dp', 'ctx'))
- grad_ffn_gain: float32 [1024], P(('dp', 'ctx'))
- grad_w_gate: float32 [1024, 4608], P(('dp', 'ctx'), 'tp')
- grad_w_up: float32 [1024, 4608], P(('dp', 'ctx'), 'tp')
- grad_w_down: float32 [4608, 1024], P('tp', ('dp', 'ctx'))
Inputs may be any that keep to these rules, and one draw needn't show every extreme that they name: For every slot index s, at least one micro-batch has lengths[m, s] = 1024. positions[m, s, 0] = 0, and from each token to the next the position rises by 1, 2 or 3.
All inputs are finite; a program needn't handle non-finite values.
Results may differ from a plain program's by a relative error of at most 0.025.
Values may be sent and summed in bfloat16 or wider, within the bound.
No kernel may reach another device: no remote copies, remote signals or barrier semaphores. Data moves between devices by JAX's collectives and lax.ppermute only.
A program may use at most 256 MiB of HBM per device.

v0:
```python
import jax
import jax.numpy as jnp
from jax import lax
from jax.sharding import PartitionSpec as P

HEADS = 16
KV_HEADS = 8
HEAD_DIM = 64


EPSILON = 1e-05
ROPE_BASE = 1000000.0
MASKED = -1e30


def norm_scale(vector):
    return lax.rsqrt(jnp.mean(vector * vector, -1, keepdims=True) + EPSILON)


def norm_back(vector, factor, gain, upstream):
    weighted = upstream * gain
    grad_vector = factor * weighted - vector * factor * factor * factor * jnp.mean(
        vector * weighted, -1, keepdims=True
    )
    return (grad_vector, upstream * vector * factor)


def rope_tables(offset_row, width):
    inverse = 1.0 / ROPE_BASE ** (jnp.arange(0, width, 2, dtype=jnp.float32) / width)
    angles = offset_row.astype(jnp.float32)[:, None] * inverse[None, :]
    angles = jnp.concatenate([angles, angles], -1)
    return (jnp.cos(angles)[:, None, :], jnp.sin(angles)[:, None, :])


def half_turn(vector):
    middle_index = vector.shape[-1] // 2
    return jnp.concatenate([-vector[..., middle_index:], vector[..., :middle_index]], -1)


def half_turn_back(vector):
    middle_index = vector.shape[-1] // 2
    return jnp.concatenate([vector[..., middle_index:], -vector[..., :middle_index]], -1)


def body(
    hidden_in,
    lengths,
    positions,
    attn_gain,
    w_query,
    w_key,
    w_value,
    q_gain,
    k_gain,
    w_output,
    ffn_gain,
    w_gate,
    w_up,
    w_down,
    grad_out,
):
    micro_count = hidden_in.shape[0]
    tok_rows = hidden_in.shape[2]
    d_model = hidden_in.shape[3]
    kv_local = KV_HEADS // lax.axis_size("tp")
    heads_local = HEADS // lax.axis_size("tp")
    group = HEADS // KV_HEADS
    length = tok_rows * lax.axis_size("ctx")
    score_scale = HEAD_DIM ** (-0.5)
    query_norm_gain = q_gain.astype(jnp.float32)
    key_norm_gain = k_gain.astype(jnp.float32)
    query_index = lax.axis_index("ctx") * tok_rows + jnp.arange(tok_rows, dtype=jnp.int32)
    key_index = jnp.arange(length, dtype=jnp.int32)
    acc_attn_gain = jnp.zeros((d_model,), jnp.float32)
    acc_query = jnp.zeros((d_model, w_query.shape[1]), jnp.float32)
    acc_key = jnp.zeros((d_model, w_key.shape[1]), jnp.float32)
    acc_value = jnp.zeros((d_model, w_value.shape[1]), jnp.float32)
    acc_output = jnp.zeros((w_output.shape[0], d_model), jnp.float32)
    acc_ffn_gain = jnp.zeros((d_model,), jnp.float32)
    acc_gate = jnp.zeros((d_model, w_gate.shape[1]), jnp.float32)
    acc_up = jnp.zeros((d_model, w_up.shape[1]), jnp.float32)
    acc_down = jnp.zeros((w_down.shape[0], d_model), jnp.float32)
    acc_q_gain = jnp.zeros((HEAD_DIM,), jnp.float32)
    acc_k_gain = jnp.zeros((HEAD_DIM,), jnp.float32)
    results = []
    input_grads = []
    for micro_index in range(micro_count):
        gathered = (
            lax.all_gather(attn_gain, ("dp", "ctx"), axis=0, tiled=True),
            lax.all_gather(w_query, ("dp", "ctx"), axis=0, tiled=True),
            lax.all_gather(w_key, ("dp", "ctx"), axis=0, tiled=True),
            lax.all_gather(w_value, ("dp", "ctx"), axis=0, tiled=True),
            lax.all_gather(w_output, ("dp", "ctx"), axis=1, tiled=True),
            lax.all_gather(ffn_gain, ("dp", "ctx"), axis=0, tiled=True),
            lax.all_gather(w_gate, ("dp", "ctx"), axis=0, tiled=True),
            lax.all_gather(w_up, ("dp", "ctx"), axis=0, tiled=True),
            lax.all_gather(w_down, ("dp", "ctx"), axis=1, tiled=True),
        )
        gain_attn, wq_full, wk_full, wv_full, wo_full, gain_ffn, wg_full, wu_full, wd_full = (
            gathered
        )
        gain_attn = gain_attn.astype(jnp.float32)
        gain_ffn = gain_ffn.astype(jnp.float32)
        stream = hidden_in[micro_index, 0].astype(jnp.float32)
        cotangent = grad_out[micro_index, 0]
        valid_length = lengths[micro_index, 0]
        cosine_table, sine_table = rope_tables(positions[micro_index, 0], HEAD_DIM)
        visible = (key_index[None, :] <= query_index[:, None]) & (key_index[None, :] < valid_length)
        attn_factor = norm_scale(stream)
        normed = (stream * attn_factor * gain_attn).astype(jnp.bfloat16)
        q_raw = jnp.dot(normed, wq_full, preferred_element_type=jnp.float32).reshape(
            tok_rows, heads_local, HEAD_DIM
        )
        k_raw = jnp.dot(normed, wk_full, preferred_element_type=jnp.float32).reshape(
            tok_rows, kv_local, HEAD_DIM
        )
        values = jnp.dot(normed, wv_full, preferred_element_type=jnp.float32).astype(jnp.bfloat16)
        query_factor = norm_scale(q_raw)
        key_factor = norm_scale(k_raw)
        query_normed = q_raw * query_factor * query_norm_gain
        key_normed = k_raw * key_factor * key_norm_gain
        queries = (query_normed * cosine_table + half_turn(query_normed) * sine_table).astype(
            jnp.bfloat16
        )
        keys = (key_normed * cosine_table + half_turn(key_normed) * sine_table).astype(jnp.bfloat16)
        keys_all, values_all = (
            lax.all_gather(keys.reshape(tok_rows, kv_local * HEAD_DIM), "ctx", axis=0, tiled=True),
            lax.all_gather(values, "ctx", axis=0, tiled=True),
        )
        query_heads = queries.reshape(tok_rows, kv_local, group, HEAD_DIM).transpose(1, 2, 0, 3)
        key_heads = keys_all.reshape(length, kv_local, HEAD_DIM).transpose(1, 0, 2)
        value_heads = values_all.reshape(length, kv_local, HEAD_DIM).transpose(1, 0, 2)

        def scores_of(query_head, key_head):
            scores = (
                jnp.einsum("gtd,jd->gtj", query_head, key_head, preferred_element_type=jnp.float32)
                * score_scale
            )
            return jnp.where(visible[None], scores, MASKED)

        def attend(bundle):
            query_head, key_head, value_head = bundle
            scores = scores_of(query_head, key_head)
            row_max = jnp.max(scores, -1, keepdims=True)
            exp_scores = jnp.exp(scores - row_max)
            row_total = jnp.sum(exp_scores, -1, keepdims=True)
            attn_probs = exp_scores / row_total
            mixed_head = jnp.einsum(
                "gtj,jd->gtd",
                attn_probs.astype(jnp.bfloat16),
                value_head,
                preferred_element_type=jnp.float32,
            )
            return (mixed_head.astype(jnp.bfloat16), row_max[..., 0] + jnp.log(row_total[..., 0]))

        mixed_heads, log_totals = lax.map(attend, (query_heads, key_heads, value_heads))
        mixed = mixed_heads.transpose(2, 0, 1, 3).reshape(tok_rows, heads_local * HEAD_DIM)
        attn_branch = lax.psum(
            jnp.dot(mixed, wo_full, preferred_element_type=jnp.float32).astype(jnp.bfloat16), "tp"
        ).astype(jnp.float32)
        middle = stream + attn_branch
        ffn_factor = norm_scale(middle)
        ffn_in = (middle * ffn_factor * gain_ffn).astype(jnp.bfloat16)
        gate_pre = jnp.dot(ffn_in, wg_full, preferred_element_type=jnp.float32)
        up_pre = jnp.dot(ffn_in, wu_full, preferred_element_type=jnp.float32)
        sigmoid_gate = jax.nn.sigmoid(gate_pre)
        activated = gate_pre * sigmoid_gate
        hidden_act = (activated * up_pre).astype(jnp.bfloat16)
        ffn_branch = lax.psum(
            jnp.dot(hidden_act, wd_full, preferred_element_type=jnp.float32).astype(jnp.bfloat16),
            "tp",
        ).astype(jnp.float32)
        results.append((middle + ffn_branch).astype(jnp.bfloat16))
        grad_hidden_act = jnp.dot(cotangent, wd_full.T, preferred_element_type=jnp.float32)
        acc_down = acc_down + jnp.dot(hidden_act.T, cotangent, preferred_element_type=jnp.float32)
        grad_gate = (
            grad_hidden_act * up_pre * sigmoid_gate * (1.0 + gate_pre * (1.0 - sigmoid_gate))
        ).astype(jnp.bfloat16)
        grad_up = (grad_hidden_act * activated).astype(jnp.bfloat16)
        acc_gate = acc_gate + jnp.dot(ffn_in.T, grad_gate, preferred_element_type=jnp.float32)
        acc_up = acc_up + jnp.dot(ffn_in.T, grad_up, preferred_element_type=jnp.float32)
        partial_ffn = jnp.dot(grad_gate, wg_full.T, preferred_element_type=jnp.float32) + jnp.dot(
            grad_up, wu_full.T, preferred_element_type=jnp.float32
        )
        grad_ffn_in = lax.psum(partial_ffn.astype(jnp.bfloat16), "tp").astype(jnp.float32)
        grad_from_ffn, gain_terms = norm_back(middle, ffn_factor, gain_ffn, grad_ffn_in)
        acc_ffn_gain = acc_ffn_gain + jnp.sum(gain_terms, 0)
        grad_middle = cotangent.astype(jnp.float32) + grad_from_ffn
        grad_attn = grad_middle.astype(jnp.bfloat16)
        acc_output = acc_output + jnp.dot(mixed.T, grad_attn, preferred_element_type=jnp.float32)
        grad_mixed = jnp.dot(grad_attn, wo_full.T, preferred_element_type=jnp.float32).astype(
            jnp.bfloat16
        )
        grad_mixed_heads = grad_mixed.reshape(tok_rows, kv_local, group, HEAD_DIM).transpose(
            1, 2, 0, 3
        )

        def attend_back(bundle):
            query_head, key_head, value_head, grad_head, log_total = bundle
            scores = scores_of(query_head, key_head)
            attn_probs = jnp.exp(scores - log_total[..., None])
            grad_probs = jnp.einsum(
                "gtd,jd->gtj", grad_head, value_head, preferred_element_type=jnp.float32
            )
            row_delta = jnp.sum(grad_probs * attn_probs, -1, keepdims=True)
            grad_scores = (attn_probs * (grad_probs - row_delta)).astype(jnp.bfloat16)
            grad_query = (
                jnp.einsum("gtj,jd->gtd", grad_scores, key_head, preferred_element_type=jnp.float32)
                * score_scale
            )
            grad_key = (
                jnp.einsum(
                    "gtj,gtd->jd", grad_scores, query_head, preferred_element_type=jnp.float32
                )
                * score_scale
            )
            grad_value = jnp.einsum(
                "gtj,gtd->jd",
                attn_probs.astype(jnp.bfloat16),
                grad_head,
                preferred_element_type=jnp.float32,
            )
            return (grad_query, grad_key, grad_value)

        grad_query_heads, grad_key_heads, grad_value_heads = lax.map(
            attend_back, (query_heads, key_heads, value_heads, grad_mixed_heads, log_totals)
        )
        grad_keys_all = grad_key_heads.transpose(1, 0, 2).reshape(length, kv_local * HEAD_DIM)
        grad_values_all = grad_value_heads.transpose(1, 0, 2).reshape(length, kv_local * HEAD_DIM)
        grad_keys_own, grad_values_own = (
            lax.psum_scatter(grad_keys_all, "ctx", scatter_dimension=0, tiled=True),
            lax.psum_scatter(grad_values_all, "ctx", scatter_dimension=0, tiled=True),
        )
        grad_values = grad_values_own.astype(jnp.bfloat16)
        grad_key_rot = grad_keys_own.reshape(tok_rows, kv_local, HEAD_DIM)
        grad_key_normed = grad_key_rot * cosine_table + half_turn_back(grad_key_rot * sine_table)
        grad_key_raw, key_gain_terms = norm_back(k_raw, key_factor, key_norm_gain, grad_key_normed)
        acc_k_gain = acc_k_gain + jnp.sum(key_gain_terms, (0, 1))
        grad_key_raw = grad_key_raw.reshape(tok_rows, kv_local * HEAD_DIM).astype(jnp.bfloat16)
        grad_query_rot = grad_query_heads.transpose(2, 0, 1, 3).reshape(
            tok_rows, heads_local, HEAD_DIM
        )
        grad_query_normed = grad_query_rot * cosine_table + half_turn_back(
            grad_query_rot * sine_table
        )
        grad_query_raw, query_gain_terms = norm_back(
            q_raw, query_factor, query_norm_gain, grad_query_normed
        )
        acc_q_gain = acc_q_gain + jnp.sum(query_gain_terms, (0, 1))
        grad_query_raw = grad_query_raw.reshape(tok_rows, heads_local * HEAD_DIM).astype(
            jnp.bfloat16
        )
        acc_query = acc_query + jnp.dot(
            normed.T, grad_query_raw, preferred_element_type=jnp.float32
        )
        acc_key = acc_key + jnp.dot(normed.T, grad_key_raw, preferred_element_type=jnp.float32)
        acc_value = acc_value + jnp.dot(normed.T, grad_values, preferred_element_type=jnp.float32)
        partial_attn = jnp.dot(grad_query_raw, wq_full.T, preferred_element_type=jnp.float32)
        partial_attn = partial_attn + jnp.dot(
            grad_key_raw, wk_full.T, preferred_element_type=jnp.float32
        )
        partial_attn = partial_attn + jnp.dot(
            grad_values, wv_full.T, preferred_element_type=jnp.float32
        )
        grad_normed = lax.psum(partial_attn.astype(jnp.bfloat16), "tp").astype(jnp.float32)
        grad_from_attn, attn_gain_terms = norm_back(stream, attn_factor, gain_attn, grad_normed)
        acc_attn_gain = acc_attn_gain + jnp.sum(attn_gain_terms, 0)
        input_grads.append((grad_middle + grad_from_attn).astype(jnp.bfloat16))
    (
        shard_attn_gain,
        shard_query,
        shard_key,
        shard_value,
        shard_output,
        shard_ffn_gain,
        shard_gate,
        shard_up,
        shard_down,
    ) = (
        lax.psum_scatter(acc_attn_gain, ("dp", "ctx"), scatter_dimension=0, tiled=True),
        lax.psum_scatter(acc_query, ("dp", "ctx"), scatter_dimension=0, tiled=True),
        lax.psum_scatter(acc_key, ("dp", "ctx"), scatter_dimension=0, tiled=True),
        lax.psum_scatter(acc_value, ("dp", "ctx"), scatter_dimension=0, tiled=True),
        lax.psum_scatter(acc_output, ("dp", "ctx"), scatter_dimension=1, tiled=True),
        lax.psum_scatter(acc_ffn_gain, ("dp", "ctx"), scatter_dimension=0, tiled=True),
        lax.psum_scatter(acc_gate, ("dp", "ctx"), scatter_dimension=0, tiled=True),
        lax.psum_scatter(acc_up, ("dp", "ctx"), scatter_dimension=0, tiled=True),
        lax.psum_scatter(acc_down, ("dp", "ctx"), scatter_dimension=1, tiled=True),
    )
    total_q_gain, total_k_gain = lax.psum((acc_q_gain, acc_k_gain), ("dp", "ctx", "tp"))
    out_hidden = jnp.stack(results)[:, None]
    grad_hidden = jnp.stack(input_grads)[:, None]
    return (
        out_hidden,
        grad_hidden,
        shard_attn_gain,
        shard_query,
        shard_key,
        shard_value,
        total_q_gain,
        total_k_gain,
        shard_output,
        shard_ffn_gain,
        shard_gate,
        shard_up,
        shard_down,
    )


def solution(mesh):
    return jax.shard_map(
        body,
        mesh=mesh,
        in_specs=(
            P(None, "dp", "ctx", None),
            P(None, "dp"),
            P(None, "dp", "ctx"),
            P(("dp", "ctx")),
            P(("dp", "ctx"), "tp"),
            P(("dp", "ctx"), "tp"),
            P(("dp", "ctx"), "tp"),
            P(),
            P(),
            P("tp", ("dp", "ctx")),
            P(("dp", "ctx")),
            P(("dp", "ctx"), "tp"),
            P(("dp", "ctx"), "tp"),
            P("tp", ("dp", "ctx")),
            P(None, "dp", "ctx", None),
        ),
        out_specs=(
            P(None, "dp", "ctx", None),
            P(None, "dp", "ctx", None),
            P(("dp", "ctx")),
            P(("dp", "ctx"), "tp"),
            P(("dp", "ctx"), "tp"),
            P(("dp", "ctx"), "tp"),
            P(),
            P(),
            P("tp", ("dp", "ctx")),
            P(("dp", "ctx")),
            P(("dp", "ctx"), "tp"),
            P(("dp", "ctx"), "tp"),
            P("tp", ("dp", "ctx")),
        ),
        check_vma=False,
    )
```

profile of v0, /device:TPU:0, one launch (start us, length us, event | category | flops | bytes accessed | tf_op | source)
XLA Modules:
  0.0 1782.3 jit_solution(6637432957250514188)
XLA Ops:
  12.5 44.3 %all-reduce.6 = (bf16[1024]{0:T(1024)(128)(2,1)S(1)}, bf16[1024]{0:T(1024)(128)(2,1)}) all-reduce(bf16[1024]{0:T(1024)(128)(2,1)S(1)} %dynamic-update-slice, bf16[1024]{0:T(1024)(128)(2,1)S(1)} %dynamic-update-slice.1), channel_id=1, replica_groups=mesh['dp'=2,'ctx'=8,'tp'=2] {'dp','ctx'}, use_global_device_ids=true, to_apply=%add | all-reduce | flops 2048 | bytes 8192
  58.0 39.8 %all_gather.50 = bf16[1024,256]{1,0:T(8,128)(2,1)S(1)} all-gather(bf16[64,256]{1,0:T(8,128)(2,1)} %param.28), channel_id=1, replica_groups=mesh['dp'=2,'ctx'=8,'tp'=2] {'dp','ctx'}, dimensions={0}, use_global_device_ids=true | all-gather | bytes 557056 | tf_op jit(solution)/shard_map/all_gather | solution.py:91
  100.8 41.9 %all_gather.52 = bf16[1024,256]{1,0:T(8,128)(2,1)S(1)} all-gather(bf16[64,256]{1,0:T(8,128)(2,1)} %param.29), channel_id=1, replica_groups=mesh['dp'=2,'ctx'=8,'tp'=2] {'dp','ctx'}, dimensions={0}, use_global_device_ids=true | all-gather | bytes 557056 | tf_op jit(solution)/shard_map/all_gather | solution.py:92
  144.8 27.4 %all_gather.59 = bf16[1024,256]{0,1:T(8,128)(2,1)S(1)} all-gather(bf16[128,256]{0,1:T(8,128)(2,1)S(1)} %bitcast.562), channel_id=1, replica_groups=mesh['dp'=2,'ctx'=8,'tp'=2] {'ctx'}, dimensions={0}, use_global_device_ids=true | all-gather | bytes 589824 | tf_op jit(solution)/shard_map/all_gather | solution.py:127
  172.2 31.3 %all_gather.60 = bf16[1024,256]{1,0:T(8,128)(2,1)S(1)} all-gather(bf16[128,256]{1,0:T(8,128)(2,1)S(1)} %convolution_convert_fusion.8), channel_id=1, replica_groups=mesh['dp'=2,'ctx'=8,'tp'=2] {'ctx'}, dimensions={0}, use_global_device_ids=true | all-gather | bytes 589824 | tf_op jit(solution)/shard_map/all_gather | solution.py:128
  205.1 27.1 %all_gather.51 = bf16[1024,256]{0,1:T(8,128)(2,1)S(1)} all-gather(bf16[128,256]{0,1:T(8,128)(2,1)S(1)} %bitcast.563), channel_id=1, replica_groups=mesh['dp'=2,'ctx'=8,'tp'=2] {'ctx'}, dimensions={0}, use_global_device_ids=true | all-gather | bytes 589824 | tf_op jit(solution)/shard_map/all_gather | solution.py:127
  232.2 31.2 %all_gather.53 = bf16[1024,256]{1,0:T(8,128)(2,1)S(1)} all-gather(bf16[128,256]{1,0:T(8,128)(2,1)S(1)} %convolution_convert_fusion.9), channel_id=1, replica_groups=mesh['dp'=2,'ctx'=8,'tp'=2] {'ctx'}, dimensions={0}, use_global_device_ids=true | all-gather | bytes 589824 | tf_op jit(solution)/shard_map/all_gather | solution.py:128
  273.2 10.0 while.57
  284.5 5.4 while.56
  297.0 13.4 all-reduce.18.cloned.1.call-done
  313.0 82.0 %all-gather.10.cloned.1.call-done = bf16[1024,2304]{1,0:T(8,128)(2,1)} async-done(((bf16[64,2304]{1,0:T(8,128)(2,1)}), bf16[1024,2304]{1,0:T(8,128)(2,1)}) %all-gather.10.cloned.1.call-update) | async-done | bytes 4718608 | tf_op jit(solution)/shard_map/all_gather | solution.py:95
  399.1 77.8 %all-gather.12.cloned.1.call-done = bf16[1024,2304]{1,0:T(8,128)(2,1)} async-done(((bf16[64,2304]{1,0:T(8,128)(2,1)}), bf16[1024,2304]{1,0:T(8,128)(2,1)}) %all-gather.12.cloned.1.call-update) | async-done | bytes 4718608 | tf_op jit(solution)/shard_map/all_gather | solution.py:96
  484.9 74.0 %all-gather.14.cloned.1.call-done = bf16[2304,1024]{0,1:T(8,128)(2,1)} async-done(((bf16[2304,64]{0,1:T(8,128)(2,1)}), bf16[2304,1024]{0,1:T(8,128)(2,1)}) %all-gather.14.cloned.1.call-update) | async-done | bytes 4718608 | tf_op jit(solution)/shard_map/all_gather | solution.py:97
  559.0 5.1 multiply_convert_fusion.2
  577.6 17.5 all-reduce.16.cloned.1.call-done
  607.9 28.4 %while.58 = (s32[]{:T(128)}, f32[4,2,128,64]{2,3,1,0:T(8,128)}, f32[4,1024,64]{1,2,0:T(8,128)S(1)}, f32[4,1024,64]{1,2,0:T(8,128)}, bf16[4,2,128,64]{2,3,1,0:T(8...) while((s32[]{:T(128)}, f32[4,2,128,64]{2,3,1,0:T(8,128)}, ...), condition=%wide.region_24.25_spmd.clone, body=%wide.region_22.24_spmd.clone.sunk | while | flops 170475264 | bytes 9252481 | solution.py:225
  640.0 22.7 %while.59 = (s32[]{:T(128)}, f32[4,2,128,64]{2,3,1,0:T(8,128)S(1)}, f32[4,1024,64]{1,2,0:T(8,128)}, f32[4,1024,64]{1,2,0:T(8,128)}, bf16[4,2,128,64]{2,3,1,0:T(8...) while((s32[]{:T(128)}, f32[4,2,128,64]{2,3,1,0:T(8,128)S(1)}, ...), condition=%wide.region_35.36_spmd.clone, body=%wide.region_33.35_spmd.clone.sunk | while | flops 170475264 | bytes 9252481 | solution.py:225
  678.2 24.4 %reduce-scatter.12.cloned.1.call-done = f32[128,256]{0,1:T(8,128)} async-done(((f32[1024,256]{0,1:T(8,128)}), f32[128,256]{0,1:T(8,128)}) %reduce-scatter.12.cloned.1.call-update) | async-done | bytes 131088 | tf_op jit(solution)/shard_map/reduce_scatter | solution.py:231
  704.1 65.1 %reduce-scatter.16.cloned.1.call-done = f32[128,256]{0,1:T(8,128)} async-done(((f32[1024,256]{0,1:T(8,128)}), f32[128,256]{0,1:T(8,128)}) %reduce-scatter.16.cloned.1.call-update) | async-done | bytes 131088 | tf_op jit(solution)/shard_map/reduce_scatter | solution.py:231
  776.5 59.0 %reduce-scatter.18.cloned.1.call-done = f32[128,256]{0,1:T(8,128)} async-done(((f32[1024,256]{0,1:T(8,128)}), f32[128,256]{0,1:T(8,128)}) %reduce-scatter.18.cloned.1.call-update) | async-done | bytes 131088 | tf_op jit(solution)/shard_map/reduce_scatter | solution.py:232
  837.5 64.8 %reduce-scatter.14.cloned.1.call-done = f32[128,256]{0,1:T(8,128)} async-done(((f32[1024,256]{0,1:T(8,128)}), f32[128,256]{0,1:T(8,128)}) %reduce-scatter.14.cloned.1.call-update) | async-done | bytes 131088 | tf_op jit(solution)/shard_map/reduce_scatter | solution.py:232
  919.5 5.1 convolution_add_fusion.2
  927.4 5.1 convolution_add_fusion.1
  935.1 5.1 convolution_add_fusion
  941.1 41.3 %all-reduce.4 = (f32[64]{0:T(128)}, f32[64]{0:T(128)}) all-reduce(f32[64]{0:T(128)S(1)} %add.309, f32[64]{0:T(128)S(1)} %add.310), channel_id=1, replica_groups=mesh['dp'=2,'ctx'=8,'tp'=2] {'dp','ctx','tp'}, use_global_device_ids=true, to_apply=%region_50.51 | all-reduce | flops 128 | bytes 1024 | tf_op jit(solution)/shard_map/psum | solution.py:290
  983.8 40.8 %all-reduce.5 = (f32[1024]{0:T(1024)S(1)}, f32[1024]{0:T(1024)S(1)}) all-reduce(f32[1024]{0:T(1024)S(1)} %add.305, f32[1024]{0:T(1024)S(1)} %add.312), channel_id=6, replica_groups=mesh['dp'=2,'ctx'=8,'tp'=2] {'dp','ctx'}, use_global_device_ids=true, to_apply=%region_44.45.clone | all-reduce | flops 2048 | bytes 16384
  1029.2 60.4 %reduce-scatter.22.cloned.1.call-done = f32[64,256]{1,0:T(8,128)} async-done(((f32[1024,256]{1,0:T(8,128)}), f32[64,256]{1,0:T(8,128)}) %reduce-scatter.22.cloned.1.call-update) | async-done | bytes 65552 | tf_op jit(solution)/shard_map/reduce_scatter | solution.py:282
  1089.6 76.8 %reduce-scatter.24.cloned.1.call-done = f32[64,256]{1,0:T(8,128)} async-done(((f32[1024,256]{1,0:T(8,128)}), f32[64,256]{1,0:T(8,128)}) %reduce-scatter.24.cloned.1.call-update) | async-done | bytes 65552 | tf_op jit(solution)/shard_map/reduce_scatter | solution.py:283
  1166.4 80.2 %reduce-scatter.26.cloned.1.call-done = f32[512,64]{0,1:T(8,128)} async-done(((f32[512,1024]{0,1:T(8,128)}), f32[512,64]{0,1:T(8,128)}) %reduce-scatter.26.cloned.1.call-update) | async-done | bytes 131088 | tf_op jit(solution)/shard_map/reduce_scatter | solution.py:284
  1246.5 175.1 %reduce-scatter.28.cloned.1.call-done = f32[64,2304]{1,0:T(8,128)} async-done(((f32[1024,2304]{1,0:T(8,128)}), f32[64,2304]{1,0:T(8,128)}) %reduce-scatter.28.cloned.1.call-update) | async-done | bytes 589840 | tf_op jit(solution)/shard_map/reduce_scatter | solution.py:286
  1421.6 176.3 %reduce-scatter.30.cloned.1.call-done = f32[64,2304]{1,0:T(8,128)} async-done(((f32[1024,2304]{1,0:T(8,128)}), f32[64,2304]{1,0:T(8,128)}) %reduce-scatter.30.cloned.1.call-update) | async-done | bytes 589840 | tf_op jit(solution)/shard_map/reduce_scatter | solution.py:287
  1598.0 177.4 %reduce-scatter.32.cloned.1.call-done = f32[2304,64]{0,1:T(8,128)} async-done(((f32[2304,1024]{0,1:T(8,128)}), f32[2304,64]{0,1:T(8,128)}) %reduce-scatter.32.cloned.1.call-update) | async-done | bytes 589840 | tf_op jit(solution)/shard_map/reduce_scatter | solution.py:288
  (460 shorter events, 195.1 us)
Async XLA Ops:
  7.2 135.5 %copy-start.2 = (bf16[2,1,128,1024]{3,2,1,0:T(8,128)(2,1)S(1)}, bf16[2,1,128,1024]{3,2,1,0:T(8,128)(2,1)}, u32[]{:S(2)}) copy-start(bf16[2,1,128,1024]{3,2,1,0:T(8,128)(2,1)} %param.23) | copy-start | bytes 1572868
  7.2 136.1 %copy-start.89 = (bf16[64]{0:T(256)(128)(2,1)S(1)}, bf16[64]{0:T(256)(128)(2,1)}, u32[]{:S(2)}) copy-start(bf16[64]{0:T(256)(128)(2,1)} %param.30) | copy-start | bytes 388
  7.2 136.1 %copy-start.84 = (s32[2,1,128]{2,1,0:T(1,128)S(1)}, s32[2,1,128]{2,1,0:T(1,128)}, u32[]{:S(2)}) copy-start(s32[2,1,128]{2,1,0:T(1,128)} %param.25) | copy-start | bytes 3076
  7.2 136.1 %copy-start.90 = (bf16[64]{0:T(256)(128)(2,1)S(1)}, bf16[64]{0:T(256)(128)(2,1)}, u32[]{:S(2)}) copy-start(bf16[64]{0:T(256)(128)(2,1)} %param.31) | copy-start | bytes 388
  7.2 257.1 %all-gather.6.cloned.1.call-start = ((), (), s32[]{:S(2)}) async-start(), calls=%async_computation.11 | async-start | bytes 1114112 | tf_op jit(solution)/shard_map/all_gather | solution.py:90
  8.0 282.0 %all-gather.8.cloned.1.call-start = ((), (), s32[]{:S(2)}) async-start(), calls=%async_computation.12 | async-start | bytes 1114112 | tf_op jit(solution)/shard_map/all_gather | solution.py:93
  8.7 301.7 %all-reduce.18.cloned.1.call-start = ((), (), s32[]{:S(2)}) async-start(), calls=%async_computation.29 | async-start | bytes 1048576 | tf_op jit(solution)/shard_map/psum | solution.py:158
  58.0 208.6 %copy-start.73 = (f32[128]{0:T(128)}, f32[128]{0:T(128)S(1)}, u32[]{:S(2)}) copy-start(f32[128]{0:T(128)S(1)} %add_rsqrt_fusion.7) | copy-start | bytes 1540
  58.0 210.3 %copy-start.75 = (f32[128]{0:T(128)}, f32[128]{0:T(128)S(1)}, u32[]{:S(2)}) copy-start(f32[128]{0:T(128)S(1)} %add_rsqrt_fusion.5) | copy-start | bytes 1540
  295.0 99.9 %all-gather.10.cloned.1.call-start = ((), (), s32[]{:S(2)}) async-start(), calls=%async_computation.13 | async-start | bytes 5013504 | tf_op jit(solution)/shard_map/all_gather | solution.py:95
  295.6 181.3 %all-gather.12.cloned.1.call-start = ((), (), s32[]{:S(2)}) async-start(), calls=%async_computation.14 | async-start | bytes 5013504 | tf_op jit(solution)/shard_map/all_gather | solution.py:96
  296.2 262.8 %all-gather.14.cloned.1.call-start = ((), (), s32[]{:S(2)}) async-start(), calls=%async_computation.15 | async-start | bytes 5013504 | tf_op jit(solution)/shard_map/all_gather | solution.py:97
  296.7 298.4 %all-reduce.16.cloned.1.call-start = ((), (), s32[]{:S(2)}) async-start(), calls=%async_computation.28 | async-start | bytes 1048576 | tf_op jit(solution)/shard_map/psum | solution.py:185
  297.0 184.3 %copy-start.66 = (f32[1024]{0:T(1024)}, f32[1024]{0:T(1024)S(1)}, u32[]{:S(2)}) copy-start(f32[1024]{0:T(1024)S(1)} %convert_element_type.274) | copy-start | bytes 12292
  311.7 169.6 %copy-start.80 = (f32[128]{0:T(128)}, f32[128]{0:T(128)S(1)}, u32[]{:S(2)}) copy-start(f32[128]{0:T(128)S(1)} %add_rsqrt_fusion.6) | copy-start | bytes 1540
  311.7 169.6 %copy-start.81 = (f32[128]{0:T(128)}, f32[128]{0:T(128)S(1)}, u32[]{:S(2)}) copy-start(f32[128]{0:T(128)S(1)} %add_rsqrt_fusion.4) | copy-start | bytes 1540
  312.9 168.3 %copy-start.9 = (bf16[128,1024]{1,0:T(8,128)(2,1)}, bf16[128,1024]{1,0:T(8,128)(2,1)S(1)}, u32[]{:S(2)}) copy-start(bf16[128,1024]{1,0:T(8,128)(2,1)S(1)} %get-tuple-element.475) | copy-start | bytes 786436
  577.6 125.0 %reduce-scatter.12.cloned.1.call-start = ((), (), s32[]{:S(2)}) async-start(), calls=%async_computation.16 | async-start | bytes 1179648 | tf_op jit(solution)/shard_map/reduce_scatter | solution.py:231
  637.3 132.0 %reduce-scatter.16.cloned.1.call-start = ((), (), s32[]{:S(2)}) async-start(), calls=%async_computation.18 | async-start | bytes 1179648 | tf_op jit(solution)/shard_map/reduce_scatter | solution.py:231
  662.7 172.8 %reduce-scatter.18.cloned.1.call-start = ((), (), s32[]{:S(2)}) async-start(), calls=%async_computation.19 | async-start | bytes 1179648 | tf_op jit(solution)/shard_map/reduce_scatter | solution.py:232
  663.3 239.0 %reduce-scatter.14.cloned.1.call-start = ((), (), s32[]{:S(2)}) async-start(), calls=%async_computation.17 | async-start | bytes 1179648 | tf_op jit(solution)/shard_map/reduce_scatter | solution.py:232
  673.1 162.3 %copy-start.18 = (bf16[1024,256]{1,0:T(8,128)(2,1)S(1)}, bf16[1024,256]{1,0:T(8,128)(2,1)}, u32[]{:S(2)}) copy-start(bf16[1024,256]{1,0:T(8,128)(2,1)} %copy-done.17) | copy-start | bytes 1572868
  676.0 227.5 %copy-start.5 = (bf16[1024,512]{1,0:T(8,128)(2,1)S(1)}, bf16[1024,512]{1,0:T(8,128)(2,1)}, u32[]{:S(2)}) copy-start(bf16[1024,512]{1,0:T(8,128)(2,1)} %all-gather.6.cloned.1.call-done) | copy-start | bytes 3145732
  676.0 306.3 %all-reduce.14.cloned.1.call-start = ((), (), s32[]{:S(2)}) async-start(), calls=%async_computation.27 | async-start | bytes 2097152 | tf_op jit(solution)/shard_map/psum | solution.py:169
  775.3 132.9 %copy-start.74 = (f32[128]{0:T(128)S(1)}, f32[128]{0:T(128)}, u32[]{:S(2)}) copy-start(f32[128]{0:T(128)} %copy-done.73) | copy-start | bytes 1540
  908.1 121.0 %reduce-scatter.20.cloned.1.call-start = ((), (), s32[]{:S(2)}) async-start(), calls=%async_computation.20 | async-start | bytes 2228224 | tf_op jit(solution)/shard_map/reduce_scatter | solution.py:281
  910.7 178.9 %reduce-scatter.22.cloned.1.call-start = ((), (), s32[]{:S(2)}) async-start(), calls=%async_computation.21 | async-start | bytes 1114112 | tf_op jit(solution)/shard_map/reduce_scatter | solution.py:282
  912.6 253.8 %reduce-scatter.24.cloned.1.call-start = ((), (), s32[]{:S(2)}) async-start(), calls=%async_computation.22 | async-start | bytes 1114112 | tf_op jit(solution)/shard_map/reduce_scatter | solution.py:283
  914.5 332.1 %reduce-scatter.26.cloned.1.call-start = ((), (), s32[]{:S(2)}) async-start(), calls=%async_computation.23 | async-start | bytes 2228224 | tf_op jit(solution)/shard_map/reduce_scatter | solution.py:284
  916.8 504.8 %reduce-scatter.28.cloned.1.call-start = ((), (), s32[]{:S(2)}) async-start(), calls=%async_computation.24 | async-start | bytes 10027008 | tf_op jit(solution)/shard_map/reduce_scatter | solution.py:286
  924.6 673.3 %reduce-scatter.30.cloned.1.call-start = ((), (), s32[]{:S(2)}) async-start(), calls=%async_computation.25 | async-start | bytes 10027008 | tf_op jit(solution)/shard_map/reduce_scatter | solution.py:287
  932.5 842.8 %reduce-scatter.32.cloned.1.call-start = ((), (), s32[]{:S(2)}) async-start(), calls=%async_computation.26 | async-start | bytes 10027008 | tf_op jit(solution)/shard_map/reduce_scatter | solution.py:288
  (82 other events, 1914.7 us)
Sparse Core Ops, SparseCore 0:
  10.9 58.7 all-gather.5
  72.5 54.8 all-gather.7
  295.1 15.1 all-reduce.17
  313.3 81.6 all-gather.9
  397.8 79.0 all-gather.11
  479.8 79.0 all-gather.13
  577.7 17.4 all-reduce.15
  637.4 65.0 reduce-scatter.11
  706.3 62.8 reduce-scatter.15
  772.5 62.8 reduce-scatter.17
  839.3 62.9 reduce-scatter.13
  908.2 18.7 all-reduce.13
  929.9 82.3 reduce-scatter.19
  1015.1 74.4 reduce-scatter.21
  1092.3 74.0 reduce-scatter.23
  1169.2 77.3 reduce-scatter.25
  1253.6 167.9 reduce-scatter.27
  1427.7 170.1 reduce-scatter.29
  1605.2 170.1 reduce-scatter.31
where the time goes:
time: 1790 us; the launch traced here: 1780 us
  waiting for transfers between devices  1230 us (69%)
  blocking collectives  325 us (18%)
  matrix products  147 us (8%)
  other arithmetic  37.8 us (2%)
  local copies, waits for them, and re-layouts  25.9 us (1%)
    reduce_scatter x1, waiting for transfers between devices, body(): lax.psum_scatter(acc_down, ('dp', 'ctx'), scatter_dimension=1, tiled=True)  177 us
    reduce_scatter x1, waiting for transfers between devices, body(): lax.psum_scatter(acc_up, ('dp', 'ctx'), scatter_dimension=0, tiled=True)  176 us
    reduce_scatter x1, waiting for transfers between devices, body(): lax.psum_scatter(acc_gate, ('dp', 'ctx'), scatter_dimension=0, tiled=True)  175 us
    reduce_scatter x2, waiting for transfers between devices, body(): lax.psum_scatter(grad_values_all, 'ctx', scatter_dimension=0, tiled=True)  124 us
    reduce_scatter x2, waiting for transfers between devices, body(): lax.psum_scatter(grad_keys_all, 'ctx', scatter_dimension=0, tiled=True)  89.5 us
    unnamed x2, blocking collectives  85 us
    all_gather x1, waiting for transfers between devices, body(): lax.all_gather(w_gate, ('dp', 'ctx'), axis=0, tiled=True)  82 us
    reduce_scatter x1, waiting for transfers between devices, body(): lax.psum_scatter(acc_output, ('dp', 'ctx'), scatter_dimension=1, tiled=True)  80.2 us
  transfers between devices with their start and end apart: 19, of which 15 were waited for; matrix products, arithmetic and copies ran while one was open for 8% of the time, Pallas kernels for 0%

commit v1 on v0

v1 whole, which is shorter than its diff:
```python
import jax
import jax.numpy as jnp
from jax import lax
from jax.sharding import Mesh, PartitionSpec as P

HEADS = 16
KV_HEADS = 8
HEAD_DIM = 64
EPSILON = 1e-05
ROPE_BASE = 1000000.0
MASKED = -1e30
BF = jnp.bfloat16
F32 = jnp.float32


def dot(a, b, dims):
    return lax.dot_general(a, b, (dims, ((), ())), preferred_element_type=F32)


def mm(a, b):
    return dot(a, b, ((1,), (0,)))


def mm_nt(a, b):
    return dot(a, b, ((1,), (1,)))


def mm_tn(a, b):
    return dot(a, b, ((0,), (0,)))


def swap(v, axis):
    return lax.ppermute(v, axis, [(0, 1), (1, 0)])


def flip(v, axis, size, d):
    return lax.ppermute(v, axis, [(i, i ^ d) for i in range(size)])


def norm_scale(vector):
    return lax.rsqrt(jnp.mean(vector * vector, -1, keepdims=True) + EPSILON)


def norm_back(vector, factor, gain, upstream):
    weighted = upstream * gain
    return factor * weighted - vector * factor * factor * factor * jnp.mean(
        vector * weighted, -1, keepdims=True
    )


def half_turn(vector):
    middle_index = vector.shape[-1] // 2
    return jnp.concatenate([-vector[..., middle_index:], vector[..., :middle_index]], -1)


def half_turn_back(vector):
    middle_index = vector.shape[-1] // 2
    return jnp.concatenate([vector[..., middle_index:], -vector[..., :middle_index]], -1)


def in_order(parts, index):
    bit = 1
    while bit < len(parts):
        flag = (index & bit) != 0
        parts = [jnp.where(flag, parts[i ^ bit], parts[i]) for i in range(len(parts))]
        bit *= 2
    return parts


def body(
    hidden_in,
    lengths,
    positions,
    attn_gain,
    w_query,
    w_key,
    w_value,
    q_gain,
    k_gain,
    w_output,
    ffn_gain,
    w_gate,
    w_up,
    w_down,
    grad_out,
):
    X, H, B, J, T = (lax.axis_size(a) for a in ("dp", "h", "b", "j", "tp"))
    ix, ih, ib, ij, it = (lax.axis_index(a) for a in ("dp", "h", "b", "j", "tp"))
    rows = hidden_in.shape[2]
    d_model = hidden_in.shape[3]
    shard = w_query.shape[0]
    group = HEADS // KV_HEADS
    qw = group * HEAD_DIM
    fw = w_gate.shape[1] // J
    count = T * J * rows
    score_scale = HEAD_DIM ** (-0.5)

    def gather(pack):
        parts = [lax.dynamic_index_in_dim(pack, ij, 0, keepdims=False)]
        for d in range(1, J):
            piece = lax.dynamic_index_in_dim(pack, ij ^ d, 0, keepdims=False)
            parts.append(flip(piece, "j", J, d))
        own = jnp.concatenate(in_order(parts, ij), 0)
        if B > 1:
            own = lax.all_gather(own, "b", axis=0, tiled=True)
        own = jnp.concatenate(in_order([own, swap(own, "h")], ih), 0)
        return jnp.concatenate(in_order([own, swap(own, "dp")], ix), 0)

    def spread(grad):
        for axis, index in (("dp", ix), ("h", ih)):
            half = grad.reshape(2, grad.shape[0] // 2, grad.shape[1])
            give = lax.dynamic_index_in_dim(half, 1 - index, 0, keepdims=False)
            keep = lax.dynamic_index_in_dim(half, index, 0, keepdims=False)
            grad = (keep.astype(F32) + swap(give, axis).astype(F32)).astype(BF)
        if B > 1:
            grad = lax.psum_scatter(grad, "b", scatter_dimension=0, tiled=True)
        pieces = grad.reshape(J, shard, grad.shape[1])
        parts = [lax.dynamic_index_in_dim(pieces, ij, 0, keepdims=False)]
        for d in range(1, J):
            piece = lax.dynamic_index_in_dim(pieces, ij ^ d, 0, keepdims=False)
            parts.append(flip(piece, "j", J, d))
        return jnp.stack(in_order(parts, ij), 1).astype(F32)

    gains = jnp.stack([attn_gain, ffn_gain])
    parts = [gains] + [flip(gains, "j", J, d) for d in range(1, J)]
    gains = jnp.concatenate(in_order(parts, ij), 1)
    if B > 1:
        gains = lax.all_gather(gains, "b", axis=1, tiled=True)
    gains = jnp.concatenate(in_order([gains, swap(gains, "h")], ih), 1)
    gains = jnp.concatenate(in_order([gains, swap(gains, "dp")], ix), 1)
    gain_attn = gains[0].astype(F32)
    gain_ffn = gains[1].astype(F32)

    w_output_t = w_output.T
    w_down_t = w_down.T
    pack_attn = jnp.concatenate(
        [
            w_query.reshape(shard, J, qw),
            w_key.reshape(shard, J, HEAD_DIM),
            w_value.reshape(shard, J, HEAD_DIM),
            w_output_t.reshape(shard, J, qw),
        ],
        2,
    ).transpose(1, 0, 2)
    wa = gather(pack_attn)
    w_qkv = wa[:, : qw + 2 * HEAD_DIM]
    wo = wa[:, qw + 2 * HEAD_DIM :]
    wg = gather(w_gate.reshape(shard, J, fw).transpose(1, 0, 2))
    wu = gather(w_up.reshape(shard, J, fw).transpose(1, 0, 2))
    wd = gather(w_down_t.reshape(shard, J, fw).transpose(1, 0, 2))

    turn = [(0, 0), (1, 2), (2, 1), (3, 3)]

    def fetch(array):
        mine = lax.dynamic_index_in_dim(array, it, 0, keepdims=False)[0]
        return lax.ppermute(mine, ("h", "tp"), turn)

    def give_back(block):
        mine = lax.ppermute(block, ("h", "tp"), turn)
        other = swap(mine, "tp")
        return jnp.stack(in_order([mine, other], it), 0)[:, None]

    def spread_tokens(block):
        parts = [block] + [flip(block, "j", J, d) for d in range(1, J)]
        half = jnp.concatenate(parts, 0)
        return jnp.concatenate([half, swap(half, "tp")], 0)

    def sum_tokens(partial):
        half = partial.reshape(T, J, rows, d_model)
        mine = half[0].astype(F32) + swap(half[1], "tp").astype(F32)
        low = mine.astype(BF)
        total = mine[0]
        for d in range(1, J):
            total = total + flip(low[d], "j", J, d).astype(F32)
        return total

    stream = fetch(hidden_in).astype(F32)
    cot_own = fetch(grad_out)
    pos_own = fetch(positions)[None]
    pos_all = spread_tokens(pos_own).reshape(count)
    valid_length = lax.dynamic_index_in_dim(lengths[:, 0], ih, 0, keepdims=False)

    place = jnp.arange(T * J, dtype=jnp.int32)
    block_of = (it ^ (place // J)) * (B * J) + (ij ^ (place % J))
    row_of = jnp.arange(rows, dtype=jnp.int32)
    query_index = ((block_of + ib * J)[:, None] * rows + row_of[None, :]).reshape(count)
    key_index = (
        (block_of[None, :] + jnp.arange(B, dtype=jnp.int32)[:, None] * J)[..., None] * rows + row_of
    ).reshape(B * count)

    inverse = 1.0 / ROPE_BASE ** (jnp.arange(0, HEAD_DIM, 2, dtype=F32) / HEAD_DIM)
    angles = pos_all.astype(F32)[:, None] * inverse[None, :]
    cosine = jnp.cos(angles)
    sine = jnp.sin(angles)
    cosine = jnp.concatenate([cosine, cosine], -1)[:, None, :]
    sine = jnp.concatenate([sine, sine], -1)[:, None, :]

    attn_factor = norm_scale(stream)
    normed_own = (stream * attn_factor * gain_attn).astype(BF)
    normed = spread_tokens(normed_own)
    raw = mm(normed, w_qkv)
    qk_raw = raw[:, : qw + HEAD_DIM].reshape(count, group + 1, HEAD_DIM)
    qk_gain = jnp.stack([q_gain] * group + [k_gain]).astype(F32)
    qk_factor = norm_scale(qk_raw)
    qk_normed = qk_raw * qk_factor * qk_gain
    qk = (qk_normed * cosine + half_turn(qk_normed) * sine).astype(BF)
    queries = qk[:, :group].transpose(1, 0, 2)
    keys = qk[:, group]
    values = raw[:, qw + HEAD_DIM :].astype(BF)
    if B > 1:
        keys = lax.all_gather(keys, "b", axis=0, tiled=True)
        values = lax.all_gather(values, "b", axis=0, tiled=True)
    visible = (key_index[None, :] <= query_index[:, None]) & (key_index[None, :] < valid_length)

    def scores_of(query_head):
        return jnp.where(visible, mm_nt(query_head, keys) * score_scale, MASKED)

    def attend(query_head):
        scores = scores_of(query_head)
        row_max = jnp.max(scores, -1, keepdims=True)
        exp_scores = jnp.exp(scores - row_max)
        row_total = jnp.sum(exp_scores, -1, keepdims=True)
        probs = (exp_scores / row_total).astype(BF)
        return mm(probs, values).astype(BF), row_max + jnp.log(row_total)

    heads = [attend(queries[g]) for g in range(group)]
    mixed = jnp.concatenate([h[0] for h in heads], -1)
    attn_branch = sum_tokens(mm_nt(mixed, wo).astype(BF))

    middle = stream + attn_branch
    ffn_factor = norm_scale(middle)
    ffn_in = spread_tokens((middle * ffn_factor * gain_ffn).astype(BF))
    cot = spread_tokens(cot_own)
    gate_pre = mm(ffn_in, wg)
    up_pre = mm(ffn_in, wu)
    sigmoid_gate = jax.nn.sigmoid(gate_pre)
    activated = gate_pre * sigmoid_gate
    hidden_act = (activated * up_pre).astype(BF)
    grad_hidden_act = mm(cot, wd)
    grad_gate = (
        grad_hidden_act * up_pre * sigmoid_gate * (1.0 + gate_pre * (1.0 - sigmoid_gate))
    ).astype(BF)
    grad_up = (grad_hidden_act * activated).astype(BF)
    grad_ffn_in = sum_tokens((mm_nt(grad_gate, wg) + mm_nt(grad_up, wu)).astype(BF))
    ffn_branch = sum_tokens(mm_nt(hidden_act, wd).astype(BF))
    out_hidden = give_back((middle + ffn_branch).astype(BF))
    shard_down = spread(mm_tn(cot, hidden_act).astype(BF))
    shard_gate = spread(mm_tn(ffn_in, grad_gate).astype(BF))
    shard_up = spread(mm_tn(ffn_in, grad_up).astype(BF))

    grad_middle = cot_own.astype(F32) + norm_back(middle, ffn_factor, gain_ffn, grad_ffn_in)
    grad_attn = spread_tokens(grad_middle.astype(BF))
    grad_mixed = mm(grad_attn, wo).astype(BF)
    grad_wo = mm_tn(grad_attn, mixed).astype(BF)

    grad_keys = jnp.zeros((B * count, HEAD_DIM), F32)
    grad_values = jnp.zeros((B * count, HEAD_DIM), F32)
    grad_queries = []
    for g in range(group):
        probs = jnp.exp(scores_of(queries[g]) - heads[g][1])
        grad_head = grad_mixed[:, g * HEAD_DIM : (g + 1) * HEAD_DIM]
        grad_probs = mm_nt(grad_head, values)
        row_delta = jnp.sum(grad_probs * probs, -1, keepdims=True)
        grad_scores = (probs * (grad_probs - row_delta)).astype(BF)
        grad_queries.append(mm(grad_scores, keys) * score_scale)
        grad_keys = grad_keys + mm_tn(grad_scores, queries[g]) * score_scale
        grad_values = grad_values + mm_tn(probs.astype(BF), grad_head)
    if B > 1:
        grad_keys = lax.psum_scatter(grad_keys, "b", scatter_dimension=0, tiled=True)
        grad_values = lax.psum_scatter(grad_values, "b", scatter_dimension=0, tiled=True)
    grad_rot = jnp.stack(grad_queries + [grad_keys], 1)
    grad_normed = grad_rot * cosine + half_turn_back(grad_rot * sine)
    grad_qk_raw = norm_back(qk_raw, qk_factor, qk_gain, grad_normed)
    terms = jnp.sum(grad_normed * qk_raw * qk_factor, 0)
    totals = jnp.stack([jnp.sum(terms[:group], 0), terms[group]])
    grad_raw = jnp.concatenate(
        [grad_qk_raw.reshape(count, qw + HEAD_DIM), grad_values], 1
    ).astype(BF)
    grad_wqkv = mm_tn(normed, grad_raw).astype(BF)
    shard_attn = spread(jnp.concatenate([grad_wqkv, grad_wo], 1))
    grad_normed_own = sum_tokens(mm_nt(grad_raw, w_qkv).astype(BF))
    grad_stream = grad_middle + norm_back(stream, attn_factor, gain_attn, grad_normed_own)
    grad_hidden = give_back(grad_stream.astype(BF))

    for axis in ("tp", "dp", "h"):
        totals = totals + swap(totals, axis)
    bit = 1
    while bit < J:
        totals = totals + flip(totals, "j", J, bit)
        bit *= 2
    if B > 1:
        totals = lax.psum(totals, "b")

    shard_query = shard_attn[:, :, :qw].reshape(shard, J * qw)
    shard_key = shard_attn[:, :, qw : qw + HEAD_DIM].reshape(shard, J * HEAD_DIM)
    shard_value = shard_attn[:, :, qw + HEAD_DIM : qw + 2 * HEAD_DIM].reshape(shard, J * HEAD_DIM)
    shard_output = shard_attn[:, :, qw + 2 * HEAD_DIM :].reshape(shard, J * qw)
    shard_gate = shard_gate.reshape(shard, J * fw)
    shard_up = shard_up.reshape(shard, J * fw)
    shard_down = shard_down.reshape(shard, J * fw)

    sum_attn = (
        jnp.sum(shard_query * w_query.astype(F32), 1)
        + jnp.sum(shard_key * w_key.astype(F32), 1)
        + jnp.sum(shard_value * w_value.astype(F32), 1)
    )
    sum_ffn = jnp.sum(shard_gate * w_gate.astype(F32), 1) + jnp.sum(
        shard_up * w_up.astype(F32), 1
    )
    sums = jnp.stack([sum_attn, sum_ffn])
    sums = (sums + swap(sums, "tp")) / jnp.stack([attn_gain, ffn_gain]).astype(F32)

    return (
        out_hidden,
        grad_hidden,
        sums[0],
        shard_query,
        shard_key,
        shard_value,
        totals[0],
        totals[1],
        shard_output.T,
        sums[1],
        shard_gate,
        shard_up,
        shard_down.T,
    )


def solution(mesh):
    places = KV_HEADS // mesh.shape["tp"]

    def run(*args):
        micro = args[0].shape[0]
        shape = (mesh.shape["dp"], micro, mesh.shape["ctx"] // (micro * places), places)
        fine = Mesh(
            mesh.devices.reshape(*shape, mesh.shape["tp"]), ("dp", "h", "b", "j", "tp")
        )
        ctx = ("h", "b", "j")
        rows = ("dp", "h", "b", "j")
        tokens = P(None, "dp", ctx, None)
        return jax.shard_map(
            body,
            mesh=fine,
            in_specs=(
                tokens,
                P(None, "dp"),
                P(None, "dp", ctx),
                P(rows),
                P(rows, "tp"),
                P(rows, "tp"),
                P(rows, "tp"),
                P(),
                P(),
                P("tp", rows),
                P(rows),
                P(rows, "tp"),
                P(rows, "tp"),
                P("tp", rows),
                tokens,
            ),
            out_specs=(
                tokens,
                tokens,
                P(rows),
                P(rows, "tp"),
                P(rows, "tp"),
                P(rows, "tp"),
                P(),
                P(),
                P("tp", rows),
                P(rows),
                P(rows, "tp"),
                P(rows, "tp"),
                P("tp", rows),
            ),
            check_vma=False,
        )(*args)

    return run
```

time: 1790 us -> 476 us (0.27)
  waiting for transfers between devices: 1230 us -> 134 us
  blocking collectives: 325 us -> 0 us
  starting transfers between devices: 1.4 us -> 119 us
  matrix products: 147 us -> 45.2 us
  local copies, waits for them, and re-layouts: 25.9 us -> 109 us
  other arithmetic: 37.8 us -> 58.9 us
    reduce_scatter x11 -> x0, waiting for transfers between devices: 960 us -> none  [the longest x1 177 us: body(): lax.psum_scatter(acc_down, ('dp', 'ctx'), scatter_dimension=1, tiled=True)]
    all_gather x5 -> x0, waiting for transfers between devices: 234 us -> none  [the longest x1 82 us: body(): lax.all_gather(w_gate, ('dp', 'ctx'), axis=0, tiled=True)]
    all_gather x6 -> x0, blocking collectives: 199 us -> none  [the longest x2 62.5 us: body(): lax.all_gather(values, 'ctx', axis=0, tiled=True)]
    ppermute x0 -> x94, waiting for transfers between devices: none -> 134 us  [the longest x33 72.7 us: swap(): return lax.ppermute(v, axis, [(0, 1), (1, 0)])]
    ppermute x0 -> x94, starting transfers between devices: none -> 119 us  [the longest x56 66.6 us: flip(): return lax.ppermute(v, axis, [(i, i ^ d) for i in range(size)])]
    dot_general x98 -> x27, matrix products: 147 us -> 45.2 us  [dot(): return lax.dot_general(a, b, (dims, ((), ())), preferred_element_type=F32)]
    unnamed x2 -> x0, blocking collectives: 85 us -> none
    psum x1 -> x0, blocking collectives: 41.3 us -> none  [body(): lax.psum((acc_q_gain, acc_k_gain), ('dp', 'ctx', 'tp'))]
  transfers between devices with their start and end apart: 19 -> 94, of which waited for: 15 -> 32; matrix products, arithmetic and copies ran while one was open for 8% -> 35% of each run, Pallas kernels for 0% -> 0%
where the time goes in v1:
time: 476 us; the launch traced here: 469 us
  waiting for transfers between devices  134 us (28%)
  starting transfers between devices  119 us (25%)
  local copies, waits for them, and re-layouts  109 us (23%)
  other arithmetic  58.9 us (12%)
  matrix products  45.2 us (9%)
    ppermute x33, waiting for transfers between devices, swap(): return lax.ppermute(v, axis, [(0, 1), (1, 0)])  72.7 us
    ppermute x56, starting transfers between devices, flip(): return lax.ppermute(v, axis, [(i, i ^ d) for i in range(size)])  66.6 us
    ppermute x56, waiting for transfers between devices, flip(): return lax.ppermute(v, axis, [(i, i ^ d) for i in range(size)])  61.2 us
    dot_general x27, matrix products, dot(): return lax.dot_general(a, b, (dims, ((), ())), preferred_element_type=F32)  45.2 us
    ppermute x33, starting transfers between devices, swap(): return lax.ppermute(v, axis, [(0, 1), (1, 0)])  45.1 us
    unnamed x252, local copies, waits for them, and re-layouts  23.6 us
    reshape x7, local copies, waits for them, and re-layouts, spread(): half = grad.reshape(2, grad.shape[0] // 2, grad.shape[1])  16.9 us
    dynamic_slice x6, local copies, waits for them, and re-layouts, spread(): keep = lax.dynamic_index_in_dim(half, index, 0, keepdims=False)  15.7 us
  transfers between devices with their start and end apart: 94, of which 32 were waited for; matrix products, arithmetic and copies ran while one was open for 35% of the time, Pallas kernels for 0%

profile of v1, /device:TPU:0, one launch (start us, length us, event | category | flops | bytes accessed | tf_op | source)
XLA Modules:
  0.0 468.7 jit_solution(17524854363218219183)
XLA Ops:
  1.4 4.0 collective-permute-start.1
  30.9 7.5 %collective-permute-start.4 = (bf16[2,256]{1,0:T(2,128)(2,1)S(1)}, bf16[2,256]{1,0:T(2,128)(2,1)S(1)}, u32[]{:S(2)}, u32[]{:S(2)}) collective-permute-start(bf16[2,256]{1,0:T(2,128)(2,1)S(1)} %pad_maximum_fusion.35), channel_id=1, source_target_pairs={{0,8},{8,0},{1,9},{9,1},{2,10},{10,2},{3,11},{11,3},{4,12},{12,4},... | collective-permute-start | bytes 3080 | tf_op jit(solution)/shard_map/ppermute | solution.py:33
  56.2 3.8 collective-permute-start.49
  60.1 3.8 collective-permute-start.13
  64.2 24.5 %collective-permute-done.13 = bf16[256,384]{1,0:T(8,128)(2,1)S(1)} collective-permute-done((bf16[256,384]{1,0:T(8,128)(2,1)S(1)}, bf16[256,384]{1,0:T(8,128)(2,1)S(1)}, u32[]{:S(2)}, u32[]{:S(2)}) %collective-permute-start.13) | collective-permute-done | bytes 196640 | tf_op jit(solution)/shard_map/ppermute | solution.py:33
  98.6 10.9 %collective-permute-done.7 = bf16[128,1024]{1,0:T(8,128)(2,1)S(1)} collective-permute-done((bf16[128,1024]{1,0:T(8,128)(2,1)S(1)}, bf16[128,1024]{1,0:T(8,128)(2,1)S(1)}, u32[]{:S(2)}, u32[]{:S(2)}) %collective-permute-start.7) | collective-permute-done | bytes 262176 | tf_op jit(solution)/shard_map/ppermute | solution.py:37
  110.9 4.3 collective-permute-done.8
  164.0 3.3 collective-permute-done.37
  169.4 10.1 %collective-permute-done.42 = bf16[512,576]{0,1:T(8,128)(2,1)} collective-permute-done((bf16[512,576]{0,1:T(8,128)(2,1)}, bf16[512,576]{0,1:T(8,128)(2,1)}, u32[]{:S(2)}, u32[]{:S(2)}) %collective-permute-start.42) | collective-permute-done | bytes 589856 | tf_op jit(solution)/shard_map/ppermute | solution.py:33
  189.6 4.5 collective-permute-done.21
  195.7 4.9 %collective-permute-done.23 = bf16[128,1024]{1,0:T(8,128)(2,1)S(1)} collective-permute-done((bf16[128,1024]{1,0:T(8,128)(2,1)S(1)}, bf16[128,1024]{1,0:T(8,128)(2,1)S(1)}, u32[]{:S(2)}, u32[]{:S(2)}) %collective-permute-start.23) | collective-permute-done | bytes 262176 | tf_op jit(solution)/shard_map/ppermute | solution.py:37
  205.5 4.0 collective-permute-done.24
  211.2 3.5 collective-permute-done.26
  222.5 3.6 multiply_convert_fusion.3
  226.1 4.0 convolution_convert_fusion.3
  230.1 3.2 convolution_convert_fusion.1
  235.8 4.0 fusion.29
  239.8 3.3 reshape.465
  243.2 3.5 constant_dynamic-slice_fusion.7
  247.3 3.3 reshape.469
  250.6 3.5 constant_dynamic-slice_fusion.3
  265.1 3.5 reshape.462
  268.7 3.5 constant_dynamic-slice_fusion.11
  280.1 3.5 collective-permute-start.79
  299.3 10.9 %collective-permute-done.79 = bf16[256,576]{0,1:T(8,128)(2,1)} collective-permute-done((bf16[256,576]{0,1:T(8,128)(2,1)S(1)}, bf16[256,576]{0,1:T(8,128)(2,1)}, u32[]{:S(2)}, u32[]{:S(2)}) %collective-permute-start.79) | collective-permute-done | bytes 294944 | tf_op jit(solution)/shard_map/ppermute | solution.py:33
  312.0 4.5 collective-permute-done.90
  346.1 4.2 collective-permute-done.57
  366.5 3.4 collective-permute-done.58
  410.1 7.6 %collective-permute-done.85 = f32[2,64]{1,0:T(2,128)S(1)} collective-permute-done((f32[2,64]{1,0:T(2,128)S(1)}, f32[2,64]{1,0:T(2,128)S(1)}, u32[]{:S(2)}, u32[]{:S(2)}) %collective-permute-start.85) | collective-permute-done | bytes 544 | tf_op jit(solution)/shard_map/ppermute | solution.py:33
  442.1 4.7 %collective-permute-done.63 = bf16[128,1024]{1,0:T(8,128)(2,1)S(1)} collective-permute-done((bf16[128,1024]{1,0:T(8,128)(2,1)S(1)}, bf16[128,1024]{1,0:T(8,128)(2,1)S(1)}, u32[]{:S(2)}, u32[]{:S(2)}) %collective-permute-start.63) | collective-permute-done | bytes 262176 | tf_op jit(solution)/shard_map/ppermute | solution.py:37
  449.3 4.3 collective-permute-done.65
  458.9 5.7 %collective-permute-start.67 = (bf16[128,1024]{1,0:T(8,128)(2,1)S(1)}, bf16[128,1024]{1,0:T(8,128)(2,1)S(1)}, u32[]{:S(2)}, u32[]{:S(2)}) collective-permute-start(bf16[128,1024]{1,0:T(8,128)(2,1)S(1)} %collective-permute-done.66), channel_id=1, source_target_pairs={{0,1},{1,0},{2,3},{3,2},{4,5},{5,4},{6,7},{7,6},{8,9},{9,8},{10,11... | collective-permute-start | bytes 786440 | tf_op jit(solution)/shard_map/ppermute | solution.py:33
  (628 shorter events, 292.1 us)
Async XLA Ops:
  1.4 22.1 %collective-permute-start.1 = (bf16[2,64]{1,0:T(2,128)(2,1)S(1)}, bf16[2,64]{1,0:T(2,128)(2,1)S(1)}, u32[]{:S(2)}, u32[]{:S(2)}) collective-permute-start(bf16[2,64]{1,0:T(2,128)(2,1)S(1)} %pad_maximum_fusion.38), channel_id=1, source_target_pairs={{0,6},{2,4},{4,2},{6,0},{1,7},{3,5},{5,3},{7,1},{8,14},{10,12},{12... | collective-permute-start | bytes 776 | tf_op jit(solution)/shard_map/ppermute | solution.py:37
  5.5 18.7 %collective-permute-start.2 = (bf16[2,64]{1,0:T(2,128)(2,1)S(1)}, bf16[2,64]{1,0:T(2,128)(2,1)S(1)}, u32[]{:S(2)}, u32[]{:S(2)}) collective-permute-start(bf16[2,64]{1,0:T(2,128)(2,1)S(1)} %pad_maximum_fusion.38), channel_id=1, source_target_pairs={{0,4},{2,6},{4,0},{6,2},{1,5},{3,7},{5,1},{7,3},{8,12},{10,14},{12... | collective-permute-start | bytes 776 | tf_op jit(solution)/shard_map/ppermute | solution.py:37
  5.9 18.3 %collective-permute-start.3 = (bf16[2,64]{1,0:T(2,128)(2,1)S(1)}, bf16[2,64]{1,0:T(2,128)(2,1)S(1)}, u32[]{:S(2)}, u32[]{:S(2)}) collective-permute-start(bf16[2,64]{1,0:T(2,128)(2,1)S(1)} %pad_maximum_fusion.38), channel_id=1, source_target_pairs={{0,2},{2,0},{4,6},{6,4},{1,3},{3,1},{5,7},{7,5},{8,10},{10,8},{12,... | collective-permute-start | bytes 776 | tf_op jit(solution)/shard_map/ppermute | solution.py:37
  8.2 42.2 %collective-permute-start.28 = (bf16[64,576]{1,0:T(8,128)(2,1)S(1)}, bf16[64,576]{1,0:T(8,128)(2,1)S(1)}, u32[]{:S(2)}, u32[]{:S(2)}) collective-permute-start(bf16[64,576]{1,0:T(8,128)(2,1)S(1)} %bitcast.492), channel_id=1, source_target_pairs={{0,6},{2,4},{4,2},{6,0},{1,7},{3,5},{5,3},{7,1},{8,14},{10,12},{12... | collective-permute-start | bytes 221192 | tf_op jit(solution)/shard_map/ppermute | solution.py:37
  11.2 40.6 %collective-permute-start.29 = (bf16[64,576]{1,0:T(8,128)(2,1)S(1)}, bf16[64,576]{1,0:T(8,128)(2,1)S(1)}, u32[]{:S(2)}, u32[]{:S(2)}) collective-permute-start(bf16[64,576]{1,0:T(8,128)(2,1)S(1)} %bitcast.491), channel_id=1, source_target_pairs={{0,4},{2,6},{4,0},{6,2},{1,5},{3,7},{5,1},{7,3},{8,12},{10,14},{12... | collective-permute-start | bytes 221192 | tf_op jit(solution)/shard_map/ppermute | solution.py:37
  27.9 18.9 %collective-permute-start.10 = (bf16[64,384]{1,0:T(8,128)(2,1)}, bf16[64,384]{1,0:T(8,128)(2,1)S(1)}, u32[]{:S(2)}, u32[]{:S(2)}) collective-permute-start(bf16[64,384]{1,0:T(8,128)(2,1)} %bitcast.463), channel_id=1, source_target_pairs={{0,6},{2,4},{4,2},{6,0},{1,7},{3,5},{5,3},{7,1},{8,14},{10,12},{12... | collective-permute-start | bytes 147464 | tf_op jit(solution)/shard_map/ppermute | solution.py:37
  51.8 37.0 %collective-permute-start = (bf16[128,1024]{1,0:T(8,128)(2,1)S(1)}, bf16[128,1024]{1,0:T(8,128)(2,1)S(1)}, u32[]{:S(2)}, u32[]{:S(2)}) collective-permute-start(bf16[128,1024]{1,0:T(8,128)(2,1)S(1)} %dynamic-slice_bitcast_fusion.2), channel_id=1, source_target_pairs={{0,0},{1,8},{8,1},{9,9},{2,2},{3,10},{10,3},{11,11},{4,4},{5,12},{... | collective-permute-start | bytes 786440 | tf_op jit(solution)/shard_map/ppermute | solution.py:156
  56.2 38.1 %collective-permute-start.49 = (bf16[128,1024]{1,0:T(8,128)(2,1)}, bf16[128,1024]{1,0:T(8,128)(2,1)}, u32[]{:S(2)}, u32[]{:S(2)}) collective-permute-start(bf16[128,1024]{1,0:T(8,128)(2,1)} %dynamic-slice_bitcast_fusion.1), channel_id=1, source_target_pairs={{0,0},{1,8},{8,1},{9,9},{2,2},{3,10},{10,3},{11,11},{4,4},{5,12},{... | collective-permute-start | bytes 786440 | tf_op jit(solution)/shard_map/ppermute | solution.py:156
  60.1 28.6 %collective-permute-start.13 = (bf16[256,384]{1,0:T(8,128)(2,1)S(1)}, bf16[256,384]{1,0:T(8,128)(2,1)S(1)}, u32[]{:S(2)}, u32[]{:S(2)}) collective-permute-start(bf16[256,384]{1,0:T(8,128)(2,1)S(1)} %pad_maximum_fusion.30), channel_id=1, source_target_pairs={{0,8},{8,0},{1,9},{9,1},{2,10},{10,2},{3,11},{11,3},{4,12},{12,4},... | collective-permute-start | bytes 589832 | tf_op jit(solution)/shard_map/ppermute | solution.py:33
  63.9 30.2 %collective-permute-start.31 = (bf16[256,576]{1,0:T(8,128)(2,1)S(1)}, bf16[256,576]{1,0:T(8,128)(2,1)S(1)}, u32[]{:S(2)}, u32[]{:S(2)}) collective-permute-start(bf16[256,576]{1,0:T(8,128)(2,1)S(1)} %pad_maximum_fusion.22), channel_id=1, source_target_pairs={{0,8},{8,0},{1,9},{9,1},{2,10},{10,2},{3,11},{11,3},{4,12},{12,4},... | collective-permute-start | bytes 884744 | tf_op jit(solution)/shard_map/ppermute | solution.py:33
  91.3 18.2 %collective-permute-start.7 = (bf16[128,1024]{1,0:T(8,128)(2,1)S(1)}, bf16[128,1024]{1,0:T(8,128)(2,1)S(1)}, u32[]{:S(2)}, u32[]{:S(2)}) collective-permute-start(bf16[128,1024]{1,0:T(8,128)(2,1)S(1)} %get-tuple-element.41), channel_id=1, source_target_pairs={{0,4},{2,6},{4,0},{6,2},{1,5},{3,7},{5,1},{7,3},{8,12},{10,14},{12... | collective-permute-start | bytes 786440 | tf_op jit(solution)/shard_map/ppermute | solution.py:37
  91.3 23.9 %collective-permute-start.8 = (bf16[128,1024]{1,0:T(8,128)(2,1)S(1)}, bf16[128,1024]{1,0:T(8,128)(2,1)S(1)}, u32[]{:S(2)}, u32[]{:S(2)}) collective-permute-start(bf16[128,1024]{1,0:T(8,128)(2,1)S(1)} %get-tuple-element.41), channel_id=1, source_target_pairs={{0,6},{2,4},{4,2},{6,0},{1,7},{3,5},{5,3},{7,1},{8,14},{10,12},{12... | collective-permute-start | bytes 786440 | tf_op jit(solution)/shard_map/ppermute | solution.py:37
  94.1 25.3 %collective-permute-start.36 = (bf16[256,576]{1,0:T(8,128)(2,1)S(1)}, bf16[256,576]{1,0:T(8,128)(2,1)S(1)}, u32[]{:S(2)}, u32[]{:S(2)}) collective-permute-start(bf16[256,576]{1,0:T(8,128)(2,1)S(1)} %pad_maximum_fusion.23), channel_id=1, source_target_pairs={{0,8},{8,0},{1,9},{9,1},{2,10},{10,2},{3,11},{11,3},{4,12},{12,4},... | collective-permute-start | bytes 884744 | tf_op jit(solution)/shard_map/ppermute | solution.py:33
  94.3 28.7 %collective-permute-start.41 = (bf16[256,576]{1,0:T(8,128)(2,1)S(1)}, bf16[256,576]{1,0:T(8,128)(2,1)S(1)}, u32[]{:S(2)}, u32[]{:S(2)}) collective-permute-start(bf16[256,576]{1,0:T(8,128)(2,1)S(1)} %pad_maximum_fusion.24), channel_id=1, source_target_pairs={{0,8},{8,0},{1,9},{9,1},{2,10},{10,2},{3,11},{11,3},{4,12},{12,4},... | collective-permute-start | bytes 884744 | tf_op jit(solution)/shard_map/ppermute | solution.py:33
  97.2 30.8 %collective-permute-start.14 = (bf16[512,384]{1,0:T(8,128)(2,1)}, bf16[512,384]{1,0:T(8,128)(2,1)}, u32[]{:S(2)}, u32[]{:S(2)}) collective-permute-start(bf16[512,384]{1,0:T(8,128)(2,1)} %pad_maximum_fusion.19), channel_id=1, source_target_pairs={{0,16},{16,0},{1,17},{17,1},{2,18},{18,2},{3,19},{19,3},{4,20},{20... | collective-permute-start | bytes 1179656 | tf_op jit(solution)/shard_map/ppermute | solution.py:33
  109.5 41.3 %collective-permute-start.50 = (bf16[128,1024]{1,0:T(8,128)(2,1)}, bf16[128,1024]{1,0:T(8,128)(2,1)}, u32[]{:S(2)}, u32[]{:S(2)}) collective-permute-start(bf16[128,1024]{1,0:T(8,128)(2,1)} %collective-permute-done.49), channel_id=1, source_target_pairs={{0,2},{2,0},{4,6},{6,4},{1,3},{3,1},{5,7},{7,5},{8,10},{10,8},{12,... | collective-permute-start | bytes 786440 | tf_op jit(solution)/shard_map/ppermute | solution.py:37
  115.2 36.0 %collective-permute-start.51 = (bf16[128,1024]{1,0:T(8,128)(2,1)}, bf16[128,1024]{1,0:T(8,128)(2,1)}, u32[]{:S(2)}, u32[]{:S(2)}) collective-permute-start(bf16[128,1024]{1,0:T(8,128)(2,1)} %collective-permute-done.49), channel_id=1, source_target_pairs={{0,4},{2,6},{4,0},{6,2},{1,5},{3,7},{5,1},{7,3},{8,12},{10,14},{12... | collective-permute-start | bytes 786440 | tf_op jit(solution)/shard_map/ppermute | solution.py:37
  122.9 31.6 %collective-permute-start.52 = (bf16[128,1024]{1,0:T(8,128)(2,1)}, bf16[128,1024]{1,0:T(8,128)(2,1)}, u32[]{:S(2)}, u32[]{:S(2)}) collective-permute-start(bf16[128,1024]{1,0:T(8,128)(2,1)} %collective-permute-done.49), channel_id=1, source_target_pairs={{0,6},{2,4},{4,2},{6,0},{1,7},{3,5},{5,3},{7,1},{8,14},{10,12},{12... | collective-permute-start | bytes 786440 | tf_op jit(solution)/shard_map/ppermute | solution.py:37
  128.0 33.8 %collective-permute-start.32 = (bf16[512,576]{0,1:T(8,128)(2,1)}, bf16[512,576]{0,1:T(8,128)(2,1)}, u32[]{:S(2)}, u32[]{:S(2)}) collective-permute-start(bf16[512,576]{0,1:T(8,128)(2,1)} %copy.93), channel_id=1, source_target_pairs={{0,16},{16,0},{1,17},{17,1},{2,18},{18,2},{3,19},{19,3},{4,20},{20... | collective-permute-start | bytes 1769480 | tf_op jit(solution)/shard_map/ppermute | solution.py:33
  144.7 38.8 %collective-permute-start.20 = (bf16[4,128,1024]{2,1,0:T(8,128)(2,1)}, bf16[4,128,1024]{2,1,0:T(8,128)(2,1)}, u32[]{:S(2)}, u32[]{:S(2)}) collective-permute-start(bf16[4,128,1024]{2,1,0:T(8,128)(2,1)} %bitcast.20), channel_id=1, source_target_pairs={{0,1},{1,0},{2,3},{3,2},{4,5},{5,4},{6,7},{7,6},{8,9},{9,8},{10,11... | collective-permute-start | bytes 3145736 | tf_op jit(solution)/shard_map/ppermute | solution.py:33
  151.3 28.2 %collective-permute-start.42 = (bf16[512,576]{0,1:T(8,128)(2,1)}, bf16[512,576]{0,1:T(8,128)(2,1)}, u32[]{:S(2)}, u32[]{:S(2)}) collective-permute-start(bf16[512,576]{0,1:T(8,128)(2,1)} %copy.99), channel_id=1, source_target_pairs={{0,16},{16,0},{1,17},{17,1},{2,18},{18,2},{3,19},{19,3},{4,20},{20... | collective-permute-start | bytes 1769480 | tf_op jit(solution)/shard_map/ppermute | solution.py:33
  156.8 58.0 %collective-permute-start.53 = (bf16[512,1024]{1,0:T(8,128)(2,1)}, bf16[512,1024]{1,0:T(8,128)(2,1)}, u32[]{:S(2)}, u32[]{:S(2)}) collective-permute-start(bf16[512,1024]{1,0:T(8,128)(2,1)} %pad_maximum_fusion.5), channel_id=1, source_target_pairs={{0,1},{1,0},{2,3},{3,2},{4,5},{5,4},{6,7},{7,6},{8,9},{9,8},{10,11... | collective-permute-start | bytes 3145736 | tf_op jit(solution)/shard_map/ppermute | solution.py:33
  246.8 27.1 %collective-permute-start.78 = (bf16[512,576]{0,1:T(8,128)(2,1)S(1)}, bf16[512,576]{0,1:T(8,128)(2,1)}, u32[]{:S(2)}, u32[]{:S(2)}) collective-permute-start(bf16[512,576]{0,1:T(8,128)(2,1)S(1)} %bitcast.485), channel_id=1, source_target_pairs={{0,16},{16,0},{1,17},{17,1},{2,18},{18,2},{3,19},{19,3},{4,20},{20... | collective-permute-start | bytes 1769480 | tf_op jit(solution)/shard_map/ppermute | solution.py:33
  255.1 28.5 %collective-permute-start.89 = (bf16[512,576]{0,1:T(8,128)(2,1)}, bf16[512,576]{0,1:T(8,128)(2,1)}, u32[]{:S(2)}, u32[]{:S(2)}) collective-permute-start(bf16[512,576]{0,1:T(8,128)(2,1)} %bitcast.444), channel_id=1, source_target_pairs={{0,16},{16,0},{1,17},{17,1},{2,18},{18,2},{3,19},{19,3},{4,20},{20... | collective-permute-start | bytes 1769480 | tf_op jit(solution)/shard_map/ppermute | solution.py:33
  258.2 60.1 %collective-permute-start.43 = (bf16[4,128,1024]{2,1,0:T(8,128)(2,1)}, bf16[4,128,1024]{2,1,0:T(8,128)(2,1)}, u32[]{:S(2)}, u32[]{:S(2)}) collective-permute-start(bf16[4,128,1024]{2,1,0:T(8,128)(2,1)} %bitcast.28), channel_id=1, source_target_pairs={{0,1},{1,0},{2,3},{3,2},{4,5},{5,4},{6,7},{7,6},{8,9},{9,8},{10,11... | collective-permute-start | bytes 3145736 | tf_op jit(solution)/shard_map/ppermute | solution.py:33
  264.6 61.2 %collective-permute-start.54 = (bf16[4,128,1024]{2,1,0:T(8,128)(2,1)}, bf16[4,128,1024]{2,1,0:T(8,128)(2,1)}, u32[]{:S(2)}, u32[]{:S(2)}) collective-permute-start(bf16[4,128,1024]{2,1,0:T(8,128)(2,1)} %bitcast.38), channel_id=1, source_target_pairs={{0,1},{1,0},{2,3},{3,2},{4,5},{5,4},{6,7},{7,6},{8,9},{9,8},{10,11... | collective-permute-start | bytes 3145736 | tf_op jit(solution)/shard_map/ppermute | solution.py:33
  280.1 30.2 %collective-permute-start.79 = (bf16[256,576]{0,1:T(8,128)(2,1)S(1)}, bf16[256,576]{0,1:T(8,128)(2,1)}, u32[]{:S(2)}, u32[]{:S(2)}) collective-permute-start(bf16[256,576]{0,1:T(8,128)(2,1)S(1)} %bitcast.488), channel_id=1, source_target_pairs={{0,8},{8,0},{1,9},{9,1},{2,10},{10,2},{3,11},{11,3},{4,12},{12,4},... | collective-permute-start | bytes 884744 | tf_op jit(solution)/shard_map/ppermute | solution.py:33
  290.5 26.1 %collective-permute-start.90 = (bf16[256,576]{0,1:T(8,128)(2,1)}, bf16[256,576]{0,1:T(8,128)(2,1)}, u32[]{:S(2)}, u32[]{:S(2)}) collective-permute-start(bf16[256,576]{0,1:T(8,128)(2,1)} %bitcast.447), channel_id=1, source_target_pairs={{0,8},{8,0},{1,9},{9,1},{2,10},{10,2},{3,11},{11,3},{4,12},{12,4},... | collective-permute-start | bytes 884744 | tf_op jit(solution)/shard_map/ppermute | solution.py:33
  296.4 32.7 %collective-permute-start.74 = (bf16[256,576]{0,1:T(8,128)(2,1)S(1)}, bf16[256,576]{0,1:T(8,128)(2,1)S(1)}, u32[]{:S(2)}, u32[]{:S(2)}) collective-permute-start(bf16[256,576]{0,1:T(8,128)(2,1)S(1)} %bitcast.487), channel_id=1, source_target_pairs={{0,8},{8,0},{1,9},{9,1},{2,10},{10,2},{3,11},{11,3},{4,12},{12,4},... | collective-permute-start | bytes 884744 | tf_op jit(solution)/shard_map/ppermute | solution.py:33
  323.0 19.6 %collective-permute-start.46 = (bf16[128,1024]{1,0:T(8,128)(2,1)}, bf16[128,1024]{1,0:T(8,128)(2,1)}, u32[]{:S(2)}, u32[]{:S(2)}) collective-permute-start(bf16[128,1024]{1,0:T(8,128)(2,1)} %get-tuple-element.82), channel_id=1, source_target_pairs={{0,6},{2,4},{4,2},{6,0},{1,7},{3,5},{5,3},{7,1},{8,14},{10,12},{12... | collective-permute-start | bytes 786440 | tf_op jit(solution)/shard_map/ppermute | solution.py:37
  331.2 19.1 %collective-permute-start.57 = (bf16[128,1024]{1,0:T(8,128)(2,1)}, bf16[128,1024]{1,0:T(8,128)(2,1)}, u32[]{:S(2)}, u32[]{:S(2)}) collective-permute-start(bf16[128,1024]{1,0:T(8,128)(2,1)} %get-tuple-element.79), channel_id=1, source_target_pairs={{0,6},{2,4},{4,2},{6,0},{1,7},{3,5},{5,3},{7,1},{8,14},{10,12},{12... | collective-permute-start | bytes 786440 | tf_op jit(solution)/shard_map/ppermute | solution.py:37
  422.8 42.4 %collective-permute-start.48 = (bf16[128,1024]{1,0:T(8,128)(2,1)}, bf16[128,1024]{1,0:T(8,128)(2,1)S(1)}, u32[]{:S(2)}, u32[]{:S(2)}) collective-permute-start(bf16[128,1024]{1,0:T(8,128)(2,1)} %collective-permute-done.47), channel_id=1, source_target_pairs={{0,1},{1,0},{2,3},{3,2},{4,5},{5,4},{6,7},{7,6},{8,9},{9,8},{10,11... | collective-permute-start | bytes 786440 | tf_op jit(solution)/shard_map/ppermute | solution.py:33
  (172 other events, 1831.3 us)
